TPU v7x, 32 devices: a whole 2x2x4 slice. The times are simulated.
32 devices in a mesh: parts: 2 (over x), blk: 4 (over y, core), rows: 4 (over z).
Axes of the slice: x: 2, y: 2, z: 4, core: 2. Of those that a mesh axis runs over, the one named last changes fastest.
Arguments:
- features: bfloat16 [8192, 512], P(('parts', 'blk', 'rows')), parts along dimension 0, may hold values from -6 to 6
- w_message: bfloat16 [512, 512], replicated, may hold values from -0.25 to 0.25
- w_update: bfloat16 [512, 512], replicated, may hold values from -0.25 to 0.25
- block_index: int32 [64, 40], P(('parts', 'blk', 'rows')), parts along dimension 0, may hold values from 0 to 31, as said below
- slot_count: int32 [64], P(('parts', 'blk', 'rows')), parts along dimension 0, may hold values from 10 to 40, as said below
- edge_count: int32 [64, 40, 128, 128], P(('parts', 'blk', 'rows')), parts along dimension 0, may hold values from 0 to 2
- cotangent: bfloat16 [8192, 512], P(('parts', 'blk', 'rows')), parts along dimension 0, may hold values from -6 to 6
Outputs:
- updated: bfloat16 [8192, 512], P(('parts', 'blk', 'rows')), parts along dimension 0
- d_features: bfloat16 [8192, 512], P(('parts', 'blk', 'rows')), parts along dimension 0
- grad_message: float32 [1024, 512], P('parts'), parts along dimension 0
- grad_update: float32 [1024, 512], P('parts'), parts along dimension 0
There are 2 independent parts, one for each index of `parts`. A program takes and returns all parts, laid end to end along the dimension named above; an argument that names none is the same for every part. Nothing has to cross between parts.
Inputs may be any that keep to these rules, and one draw needn't show every extreme that they name: `block_index`: the source blocks of a block row lie in its own region or in the two regions beside it on the periodic chain; block b lies in region b // 8. `slot_count`: some block row uses all 40 slots in every draw.
All inputs are finite; a program needn't handle non-finite values.
Results may differ from a plain program's by a relative error of at most 0.015.
Values may be sent and summed in bfloat16 or wider, within the bound.
A program may use at most 128 MiB of HBM per device.

v0:
```python
import math

import jax
import jax.numpy as jnp
from jax import lax
from jax.sharding import PartitionSpec as P


def from_behind(array, axis, by):
    devices = lax.axis_size(axis)
    return lax.ppermute(array, axis, [(i, (i + by) % devices) for i in range(devices)])


def body(features, w_message, w_update, block_index, slot_count, edge_count, cotangent):
    tile_size = edge_count.shape[2]
    feat_width = features.shape[1]
    local_blocks = block_index.shape[0]
    slot_total = block_index.shape[1]
    row_devices = lax.axis_size("rows")
    chain_size = lax.axis_size("blk")
    region_index = lax.axis_index("blk")
    region_blocks = local_blocks * row_devices
    own_hidden = jnp.dot(features, w_message, preferred_element_type=jnp.float32).astype(
        jnp.bfloat16
    )
    region_hidden = lax.all_gather(own_hidden, "rows", axis=0, tiled=True)
    before = from_behind(region_hidden, "blk", 1)
    after = from_behind(region_hidden, "blk", -1)
    window = jnp.concatenate([before, region_hidden, after], axis=0).reshape(
        3 * region_blocks, tile_size, feat_width
    )
    offsets = jnp.mod(block_index - (region_index - 1) * region_blocks, chain_size * region_blocks)
    slot_valid = jnp.arange(slot_total, dtype=jnp.int32)[None, :] < slot_count[:, None]
    counts = jnp.where(slot_valid[:, :, None, None], edge_count, jnp.int32(0))
    counts_f = counts.astype(jnp.float32)
    row_norm = jnp.sqrt(1.0 + jnp.sum(counts_f * counts_f, axis=(1, 3)))
    tiles_bf = counts.astype(jnp.bfloat16)
    sources = window[offsets]
    summed = jnp.einsum("bsij,bsjd->bid", tiles_bf, sources, preferred_element_type=jnp.float32)
    message = summed / row_norm[:, :, None]
    smooth = jax.nn.silu(message).astype(jnp.bfloat16)
    smooth_rows = smooth.reshape(-1, feat_width)
    updated = (
        features.astype(jnp.float32)
        + jnp.dot(smooth_rows, w_update, preferred_element_type=jnp.float32)
    ).astype(jnp.bfloat16)
    update_term = jnp.dot(smooth_rows.T, cotangent, preferred_element_type=jnp.float32)
    d_smooth = jnp.dot(cotangent, w_update.T, preferred_element_type=jnp.float32).reshape(
        local_blocks, tile_size, feat_width
    )
    sigmoid_m = jax.nn.sigmoid(message)
    d_message = (
        d_smooth * sigmoid_m * (1.0 + message * (1.0 - sigmoid_m)) / row_norm[:, :, None]
    ).astype(jnp.bfloat16)
    contrib = jnp.einsum("bsij,bid->bsjd", tiles_bf, d_message, preferred_element_type=jnp.float32)
    partial_value = jnp.zeros((3 * region_blocks, tile_size, feat_width), jnp.float32)
    partial_value = partial_value.at[offsets.reshape(-1)].add(
        contrib.reshape(-1, tile_size, feat_width)
    )
    partial_value = partial_value.astype(jnp.bfloat16).reshape(
        3, region_blocks * tile_size, feat_width
    )
    part_before = partial_value[0]
    part_centre = partial_value[1]
    part_after = partial_value[2]
    to_owner_before = from_behind(part_before, "blk", -1)
    to_owner_after = from_behind(part_after, "blk", 1)
    sums = (
        lax.psum_scatter(part_centre, "rows", scatter_dimension=0, tiled=True).astype(jnp.float32),
        lax.psum_scatter(to_owner_before, "rows", scatter_dimension=0, tiled=True).astype(
            jnp.float32
        ),
        lax.psum_scatter(to_owner_after, "rows", scatter_dimension=0, tiled=True).astype(
            jnp.float32
        ),
    )
    d_hidden = sums[0] + sums[1] + sums[2]
    d_hidden_bf = d_hidden.astype(jnp.bfloat16)
    d_features = (
        cotangent.astype(jnp.float32)
        + jnp.dot(d_hidden_bf, w_message.T, preferred_element_type=jnp.float32)
    ).astype(jnp.bfloat16)
    message_term = jnp.dot(features.T, d_hidden_bf, preferred_element_type=jnp.float32)
    grad_scale = 1.0 / math.sqrt(features.shape[0] * chain_size * row_devices)
    grad_message, grad_update = lax.psum((message_term, update_term), ("blk", "rows"))
    return (updated, d_features, grad_message * grad_scale, grad_update * grad_scale)


def solution(mesh):
    placed = (
        P(("parts", "blk", "rows"), None),
        P(),
        P(),
        P(("parts", "blk", "rows"), None),
        P(("parts", "blk", "rows")),
        P(("parts", "blk", "rows"), None, None, None),
        P(("parts", "blk", "rows"), None),
    )
    return jax.shard_map(
        body,
        mesh=mesh,
        in_specs=placed,
        out_specs=(
            P(("parts", "blk", "rows"), None),
            P(("parts", "blk", "rows"), None),
            P("parts", None),
            P("parts", None),
        ),
        check_vma=False,
    )
```

profile of v0, /device:TPU:0, one launch (start us, length us, event | category | flops | bytes accessed | tf_op | source)
XLA Modules:
  0.0 341.4 jit_solution(3123527141868205844)
XLA Ops:
  7.2 2.2 convolution_convert_fusion
  11.1 29.7 %all-gather.2.cloned.1.call-done = bf16[1024,512]{1,0:T(8,128)(2,1)} async-done(((bf16[256,512]{1,0:T(8,128)(2,1)}), bf16[1024,512]{1,0:T(8,128)(2,1)}) %all-gather.2.cloned.1.call-update) | async-done | bytes 1048592 | tf_op jit(solution)/shard_map/all_gather | solution.py:26
  40.8 1.7 collective-permute-start.1
  42.6 3.4 multiply_reduce_fusion
  46.4 18.3 %collective-permute-done = bf16[1024,512]{1,0:T(8,128)(2,1)S(1)} collective-permute-done((bf16[1024,512]{1,0:T(8,128)(2,1)}, bf16[1024,512]{1,0:T(8,128)(2,1)S(1)}, u32[]{:S(2)}, u32[]{:S(2)}) %collective-permute-start) | collective-permute-done | bytes 1048608 | tf_op jit(solution)/shard_map/ppermute | solution.py:11
  65.6 1.9 pad_maximum_fusion
  67.5 8.3 %gather_fusion = bf16[80,128,512]{2,1,0:T(8,128)(2,1)} fusion(bf16[24,128,512]{2,1,0:T(8,128)(2,1)} %bitcast.34, s32[1024]{0:T(1024)S(1)} %pad_clamp_fusion), kind=kCustom, calls=%fused_computation | custom fusion | bytes 20971840 | tf_op jit(solution)/shard_map/gather | solution.py:38
  75.8 6.6 %multiply_convert_fusion = (bf16[2,128,512]{2,1,0:T(8,128)(2,1)S(1)}, f32[2,128,512]{2,1,0:T(8,128)S(1)}) fusion(f32[2,128]{1,0:T(2,128)S(1)} %add_sqrt_fusion, bf16[2,40,128,512]{3,2,1,0:T(8,128)(2,1)} %bitcast.37, s32[2,40,128,128]{3,2,1,0:T(8,128)} %param.12, pred[2,40]{1,0:T(4,128)(4,1)S(1)} %iota_compare_fusion), kind=kOutput, calls=%fused_computation.18 | convolution fusion | flops 1345585152 | bytes 16516176 | tf_op jit(solution)/shard_map/bsij,bsjd->bid/dot_general | solution.py:39
  82.5 8.6 %fusion.3 = f32[2,40,128,512]{3,2,1,0:T(8,128)} fusion(s32[2,40,128,128]{3,2,1,0:T(8,128)S(1)} %bitcast.36, pred[2,40]{1,0:T(4,128)(4,1)S(1)} %iota_compare_fusion, f32[2,128,512]{2,1,0:T(8,128)S(1)} %get-tuple-element.16, f32[2,128,512]{2,1,0:T(8,128)S(1)} %bitcast.39, f32[2,128]{1,0:T(2,128)S(1)} %add_sqrt_fusion), kind=kOutput, calls=%fused_computation.13 | convolution fusion | flops 1346109440 | bytes 27264080 | tf_op jit(solution)/shard_map/bsij,bid->bsjd/dot_general | solution.py:55
  91.1 3.5 %broadcast_in_dim.27 = f32[24,128,512]{2,1,0:T(8,128)} broadcast(f32[]{:T(128)} %constant.38.clone.1), dimensions={} | broadcast | bytes 6291460 | tf_op jit(solution)/shard_map/broadcast_in_dim | solution.py:56
  94.6 45.2 %scatter_fusion = f32[24,128,512]{2,1,0:T(8,128)} fusion(f32[24,128,512]{2,1,0:T(8,128)} %broadcast_in_dim.27, s32[80]{0:T(128)S(1)} %fusion.7, f32[80,128,512]{2,1,0:T(8,128)} %bitcast.33), kind=kCustom, calls=%fused_computation.1 | custom fusion | flops 5242880 | bytes 62914880 | tf_op jit(solution)/shard_map/scatter-add | solution.py:57
  139.8 3.2 convert_element_type.50
  143.0 1.8 fusion.11
  144.9 2.5 collective-permute-start.2
  147.4 12.6 %collective-permute-done.2 = bf16[1024,512]{1,0:T(8,128)(2,1)S(1)} collective-permute-done((bf16[1024,512]{1,0:T(8,128)(2,1)}, bf16[1024,512]{1,0:T(8,128)(2,1)S(1)}, u32[]{:S(2)}, u32[]{:S(2)}) %collective-permute-start.2) | collective-permute-done | bytes 1048608 | tf_op jit(solution)/shard_map/ppermute | solution.py:11
  161.9 14.1 %collective-permute-done.3 = bf16[1024,512]{1,0:T(8,128)(2,1)S(1)} collective-permute-done((bf16[1024,512]{1,0:T(8,128)(2,1)}, bf16[1024,512]{1,0:T(8,128)(2,1)S(1)}, u32[]{:S(2)}, u32[]{:S(2)}) %collective-permute-start.3) | collective-permute-done | bytes 1048608 | tf_op jit(solution)/shard_map/ppermute | solution.py:11
  177.0 1.3 fusion.13
  178.4 22.4 %reduce-scatter.6.cloned.1.call-done = bf16[256,512]{1,0:T(8,128)(2,1)} async-done(((bf16[1024,512]{1,0:T(8,128)(2,1)}), bf16[256,512]{1,0:T(8,128)(2,1)}) %reduce-scatter.6.cloned.1.call-update) | async-done | bytes 262160 | tf_op jit(solution)/shard_map/reduce_scatter | solution.py:70
  200.8 28.6 %reduce-scatter.8.cloned.1.call-done = bf16[256,512]{1,0:T(8,128)(2,1)} async-done(((bf16[1024,512]{1,0:T(8,128)(2,1)}), bf16[256,512]{1,0:T(8,128)(2,1)}) %reduce-scatter.8.cloned.1.call-update) | async-done | bytes 262160 | tf_op jit(solution)/shard_map/reduce_scatter | solution.py:73
  229.3 2.5 convolution_bitcast_fusion
  233.9 96.6 %all-reduce.3.cloned.1.call-done = (f32[512,512]{0,1:T(8,128)}, f32[512,512]{0,1:T(8,128)}) async-done(((f32[512,512]{0,1:T(8,128)}, f32[512,512]{0,1:T(8,128)}), (f32[512,512]{0,1:T(8,128)}, f32[512,512]{0,1:T(8,128)})) %all-reduce.3.cloned.1.call-update) | async-done | bytes 2097168 | tf_op jit(solution)/shard_map/psum | solution.py:85
  330.5 1.8 broadcast_multiply_fusion
  332.3 1.3 copy.13
  333.6 1.3 copy.14
  (49 shorter events, 8.1 us)
Async XLA Ops:
  7.2 38.8 %copy-start = (bf16[512,512]{1,0:T(8,128)(2,1)S(1)}, bf16[512,512]{1,0:T(8,128)(2,1)}, u32[]{:S(2)}) copy-start(bf16[512,512]{1,0:T(8,128)(2,1)} %param.9) | copy-start | bytes 1572868
  7.2 38.8 %copy-start.1 = (bf16[256,512]{1,0:T(8,128)(2,1)S(1)}, bf16[256,512]{1,0:T(8,128)(2,1)}, u32[]{:S(2)}) copy-start(bf16[256,512]{1,0:T(8,128)(2,1)} %param.13) | copy-start | bytes 786436
  7.2 33.6 %all-gather.2.cloned.1.call-start = ((), (), s32[]{:S(2)}) async-start(), calls=%async_computation.3 | async-start | bytes 1310720 | tf_op jit(solution)/shard_map/all_gather | solution.py:26
  9.4 168.9 %reduce-scatter.4.cloned.1.call-start = ((), (), s32[]{:S(2)}) async-start(), calls=%async_computation.4 | async-start | bytes 1310720 | tf_op jit(solution)/shard_map/reduce_scatter | solution.py:69
  40.8 24.8 %copy-start.6 = (bf16[1024,512]{1,0:T(8,128)(2,1)S(1)}, bf16[1024,512]{1,0:T(8,128)(2,1)}, u32[]{:S(2)}) copy-start(bf16[1024,512]{1,0:T(8,128)(2,1)} %all-gather.2.cloned.1.call-done) | copy-start | bytes 3145732
  40.8 23.8 %collective-permute-start = (bf16[1024,512]{1,0:T(8,128)(2,1)}, bf16[1024,512]{1,0:T(8,128)(2,1)S(1)}, u32[]{:S(2)}, u32[]{:S(2)}) collective-permute-start(bf16[1024,512]{1,0:T(8,128)(2,1)} %all-gather.2.cloned.1.call-done), channel_id=1, source_target_pairs={{0,4},{4,8},{8,12},{12,0},{1,5},{5,9},{9,13},{13,1},{2,6},{6,10},{... | collective-permute-start | bytes 3145736 | tf_op jit(solution)/shard_map/ppermute | solution.py:11
  40.8 24.8 %collective-permute-start.1 = (bf16[1024,512]{1,0:T(8,128)(2,1)}, bf16[1024,512]{1,0:T(8,128)(2,1)S(1)}, u32[]{:S(2)}, u32[]{:S(2)}) collective-permute-start(bf16[1024,512]{1,0:T(8,128)(2,1)} %all-gather.2.cloned.1.call-done), channel_id=1, source_target_pairs={{0,12},{4,0},{8,4},{12,8},{1,13},{5,1},{9,5},{13,9},{2,14},{6,2},{... | collective-permute-start | bytes 3145736 | tf_op jit(solution)/shard_map/ppermute | solution.py:11
  67.5 14.9 %slice-start = ((s8[5242880]{0:T(1024)(128)(4,1)}), s8[1048576]{0:T(1024)(128)(4,1)S(1)}, s32[]{:S(2)}) async-start(s8[5242880]{0:T(1024)(128)(4,1)} %bitcast.35), calls=%async_computation.8 | async-start | bytes 2097152
  75.8 6.7 %slice-start.1 = ((s8[5242880]{0:T(1024)(128)(4,1)}), s8[4194304]{0:T(1024)(128)(4,1)S(1)}, s32[]{:S(2)}) async-start(s8[5242880]{0:T(1024)(128)(4,1)} %bitcast.35), calls=%async_computation.9 | async-start | bytes 8388608
  143.0 86.3 %copy-start.2 = (bf16[256,512]{1,0:T(8,128)(2,1)S(1)}, bf16[256,512]{1,0:T(8,128)(2,1)}, u32[]{:S(2)}) copy-start(bf16[256,512]{1,0:T(8,128)(2,1)} %param.7) | copy-start | bytes 786436
  144.8 88.0 %copy-start.3 = (bf16[512,512]{1,0:T(8,128)(2,1)S(1)}, bf16[512,512]{1,0:T(8,128)(2,1)}, u32[]{:S(2)}) copy-start(bf16[512,512]{1,0:T(8,128)(2,1)} %param.8) | copy-start | bytes 1572868
  144.9 55.9 %reduce-scatter.6.cloned.1.call-start = ((), (), s32[]{:S(2)}) async-start(), calls=%async_computation.5 | async-start | bytes 1310720 | tf_op jit(solution)/shard_map/reduce_scatter | solution.py:70
  144.9 15.1 %collective-permute-start.2 = (bf16[1024,512]{1,0:T(8,128)(2,1)}, bf16[1024,512]{1,0:T(8,128)(2,1)S(1)}, u32[]{:S(2)}, u32[]{:S(2)}) collective-permute-start(bf16[1024,512]{1,0:T(8,128)(2,1)} %bitcast.43), channel_id=1, source_target_pairs={{0,12},{4,0},{8,4},{12,8},{1,13},{5,1},{9,5},{13,9},{2,14},{6,2},{... | collective-permute-start | bytes 3145736 | tf_op jit(solution)/shard_map/ppermute | solution.py:11
  160.0 1.0 copy-start.4
  161.0 68.3 %reduce-scatter.8.cloned.1.call-start = ((), (), s32[]{:S(2)}) async-start(), calls=%async_computation.6 | async-start | bytes 1310720 | tf_op jit(solution)/shard_map/reduce_scatter | solution.py:73
  161.0 14.9 %collective-permute-start.3 = (bf16[1024,512]{1,0:T(8,128)(2,1)}, bf16[1024,512]{1,0:T(8,128)(2,1)S(1)}, u32[]{:S(2)}, u32[]{:S(2)}) collective-permute-start(bf16[1024,512]{1,0:T(8,128)(2,1)} %bitcast.42), channel_id=1, source_target_pairs={{0,4},{4,8},{8,12},{12,0},{1,5},{5,9},{9,13},{13,1},{2,6},{6,10},{... | collective-permute-start | bytes 3145736 | tf_op jit(solution)/shard_map/ppermute | solution.py:11
  176.0 1.0 copy-start.5
  177.0 153.5 %all-reduce.3.cloned.1.call-start = ((), (), s32[]{:S(2)}) async-start(), calls=%async_computation.7 | async-start | bytes 4194304 | tf_op jit(solution)/shard_map/psum | solution.py:85
  178.4 54.5 %copy-start.7 = (bf16[256,512]{1,0:T(8,128)(2,1)S(1)}, bf16[256,512]{1,0:T(8,128)(2,1)}, u32[]{:S(2)}) copy-start(bf16[256,512]{1,0:T(8,128)(2,1)} %reduce-scatter.4.cloned.1.call-done) | copy-start | bytes 786436
  200.8 32.1 %copy-start.8 = (bf16[256,512]{1,0:T(8,128)(2,1)S(1)}, bf16[256,512]{1,0:T(8,128)(2,1)}, u32[]{:S(2)}) copy-start(bf16[256,512]{1,0:T(8,128)(2,1)} %reduce-scatter.6.cloned.1.call-done) | copy-start | bytes 786436
  229.3 3.5 %copy-start.9 = (bf16[256,512]{1,0:T(8,128)(2,1)S(1)}, bf16[256,512]{1,0:T(8,128)(2,1)}, u32[]{:S(2)}) copy-start(bf16[256,512]{1,0:T(8,128)(2,1)} %reduce-scatter.8.cloned.1.call-done) | copy-start | bytes 786436
Sparse Core Ops, SparseCore 0:
  10.2 30.6 all-gather.1
  145.0 27.5 reduce-scatter.3
  175.0 25.7 reduce-scatter.5
  203.5 25.7 reduce-scatter.7
  233.8 96.6 all-reduce.2
where the time goes:
time: 342 us; the launch traced here: 341 us
  waiting for transfers between devices  223 us (65%)
  other arithmetic  56.9 us (17%)
  matrix products  23.6 us (7%)
  local copies, waits for them, and re-layouts  18.4 us (5%)
  between operations  13.9 us (4%)
  starting transfers between devices  5.21 us (2%)
    psum x1, waiting for transfers between devices, body(): lax.psum((message_term, update_term), ('blk', 'rows'))  96.6 us
    ppermute x4, waiting for transfers between devices, from_behind(): lax.ppermute(array, axis, [(i, (i + by) % devices) for i in range(devices)])  46 us
    scatter-add x1, other arithmetic, body(): partial_value.at[offsets.reshape(-1)]  45.2 us
    all_gather x1, waiting for transfers between devices, body(): region_hidden = lax.all_gather(own_hidden, 'rows', axis=0, tiled=True)  29.7 us
    reduce_scatter x1, waiting for transfers between devices, body(): lax.psum_scatter(to_owner_after, 'rows', scatter_dimension=0, tiled=True)  28.6 us
    reduce_scatter x1, waiting for transfers between devices, body(): lax.psum_scatter(to_owner_before, 'rows', scatter_dimension=0, tiled=True)  22.4 us
    dot_general x1, matrix products, body(): jnp.einsum('bsij,bid->bsjd', tiles_bf, d_message, preferred_element_type=...  8.64 us
    gather x1, local copies, waits for them, and re-layouts, body(): sources = window[offsets]  8.28 us
  transfers between devices with their start and end apart: 9, of which 8 were waited for; matrix products, arithmetic and copies ran while one was open for 3% of the time, Pallas kernels for 0%

commit v1 on v0

v1 whole, which is shorter than its diff:
```python
import functools
import math

import jax
import jax.numpy as jnp
from jax import lax
from jax.experimental import pallas as pl
from jax.experimental.pallas import tpu as pltpu
from jax.sharding import PartitionSpec as P

MESH = pl.DeviceIdType.MESH
F32 = jnp.float32
BF16 = jnp.bfloat16
SLOT_STEP = 8


def partner(z, j):
    out, bit = z, 1
    while bit <= j:
        if j & bit:
            out = out + bit * (1 - 2 * ((z // bit) % 2))
        bit *= 2
    return out


def dense_kernel(nb, region_blocks, index_ref, count_ref, edge_ref, a_ref, sq_ref):
    b = pl.program_id(0)
    step = pl.program_id(1)
    r = lax.axis_index("blk")
    tile = edge_ref.shape[2]

    @pl.when((b == 0) & (step == 0))
    def _():
        a_ref[...] = jnp.zeros_like(a_ref)
        sq_ref[...] = jnp.zeros_like(sq_ref)

    rows = pl.ds(pl.multiple_of(b * tile, tile), tile)
    used = count_ref[b]
    for i in range(edge_ref.shape[1]):
        s = step * edge_ref.shape[1] + i

        @pl.when(s < used)
        def _():
            total = nb * region_blocks
            k = lax.rem(index_ref[b, s] - (r - 1) * region_blocks + 2 * total, total)
            c = edge_ref[0, i].astype(BF16)
            a_ref[k, rows, :] += c
            sq_ref[rows, :] += c * c


def dense(block_index, slot_count, edge_count, nb, nr):
    lb, slots = block_index.shape
    tile = edge_count.shape[2]
    step = SLOT_STEP if slots % SLOT_STEP == 0 else 1
    region_blocks = lb * nr
    return pl.pallas_call(
        functools.partial(dense_kernel, nb, region_blocks),
        grid=(lb, slots // step),
        out_shape=(
            jax.ShapeDtypeStruct((3 * region_blocks, lb * tile, tile), BF16),
            jax.ShapeDtypeStruct((lb * tile, tile), BF16),
        ),
        in_specs=[
            pl.BlockSpec(memory_space=pltpu.SMEM),
            pl.BlockSpec(memory_space=pltpu.SMEM),
            pl.BlockSpec((1, step, tile, tile), lambda b, s: (b, s, 0, 0)),
        ],
        out_specs=(
            pl.BlockSpec((3 * region_blocks, lb * tile, tile), lambda b, s: (0, 0, 0)),
            pl.BlockSpec((lb * tile, tile), lambda b, s: (0, 0)),
        ),
        compiler_params=pltpu.CompilerParams(vmem_limit_bytes=32 * 1024 * 1024),
    )(block_index, slot_count, edge_count)


def layer_kernel(
    nb, nr, lb,
    a_ref, sq_ref, x_ref, cot_ref, wm_ref, wu_ref,
    upd_ref, df_ref, gout,
    xwin, qs, qr, ss, sr, acc, ds, g, grecv, hbuf, yrecv, h2, zrecv,
    s1, r1, sf, rf, sq_s, sq_r, st_s, st_r,
    sp, rp, sy, ry, sz, rz, sa, ra, sb, rb, sm, rm,
):
    z = lax.axis_index("rows")
    r = lax.axis_index("blk")
    ny = nb // 2
    c = lax.rem(r, 2)
    yy = r // 2
    mate = yy * 2 + (1 - c)
    up, down = lax.rem(r + 1, nb), lax.rem(r + nb - 1, nb)
    row_peer = [partner(z, j) for j in range(nr)]
    y_peer = [lax.rem(yy + i, ny) for i in range(ny)]
    y_from = [lax.rem(yy + ny - i, ny) for i in range(ny)]

    def copy(src, dst, send, recv, where):
        return pltpu.make_async_remote_copy(
            src_ref=src, dst_ref=dst, send_sem=send, recv_sem=recv,
            device_id=where, device_id_type=MESH,
        )

    barrier = pltpu.get_barrier_semaphore()
    peers = [{"rows": row_peer[j]} for j in range(1, nr)]
    peers += [{"blk": up}, {"blk": down}]
    peers += [{"blk": lax.rem(r + 2 * i, nb)} for i in range(1, ny)]
    for where in peers:
        pl.semaphore_signal(barrier, inc=1, device_id=where, device_id_type=MESH)
    pl.semaphore_wait(barrier, len(peers))

    sends = []

    def start(*args):
        one = copy(*args)
        one.start()
        sends.append(one)

    def forward(j):
        src = x_ref if j == 0 else xwin.at[nr + row_peer[j]]
        start(src, xwin.at[row_peer[j]], sf.at[0, j], rf.at[0, j], {"blk": up})
        start(src, xwin.at[2 * nr + row_peer[j]], sf.at[1, j], rf.at[1, j], {"blk": down})

    forward(0)
    for j in range(1, nr):
        start(x_ref, xwin.at[nr + z], s1.at[j - 1], r1.at[j - 1], {"rows": row_peer[j]})

    def tiles(side, shard):
        first = (side * nr + shard) * lb
        return jnp.concatenate([a_ref[first + i] for i in range(lb)], axis=1)

    def mm(a, b):
        return jnp.dot(a, b, preferred_element_type=F32)

    def mm_t(a, b):
        return lax.dot_general(a, b, (((0,), (0,)), ((), ())), preferred_element_type=F32)

    def mm_bt(a, b):
        return lax.dot_general(a, b, (((1,), (1,)), ((), ())), preferred_element_type=F32)

    ds[...] = mm_bt(cot_ref[...], wu_ref[...])
    acc[...] = mm(tiles(1, z), x_ref[...])
    for j in range(1, nr):
        slot = nr + row_peer[j]
        copy(x_ref, xwin.at[slot], s1.at[j - 1], r1.at[j - 1], {"rows": row_peer[j]}).wait_recv()
        forward(j)
        acc[...] += mm(tiles(1, row_peer[j]), xwin[slot])
    for j in range(nr):
        for d, side, where in ((0, 0, up), (1, 2, down)):
            slot = side * nr + row_peer[j]
            copy(x_ref, xwin.at[slot], sf.at[d, j], rf.at[d, j], {"blk": where}).wait_recv()
            acc[...] += mm(tiles(side, row_peer[j]), xwin[slot])

    inv = 1.0 / jnp.sqrt(1.0 + jnp.sum(sq_ref[...].astype(F32), axis=1, keepdims=True))
    y = acc[...].astype(BF16)
    message = mm(y, wm_ref[...]) * inv
    sig = 1.0 / (1.0 + jnp.exp(-message))
    smooth = (message * sig).astype(BF16)
    d_message = (ds[...] * sig * (1.0 + message * (1.0 - sig)) * inv).astype(BF16)
    dz = mm_bt(d_message, wm_ref[...]).astype(BF16)
    ds[...] = dz.astype(F32)

    order = list(range(1, nr)) + [0]
    for j in order:
        for d, side, where in ((0, 2, up), (1, 0, down)):
            qs[d, j] = mm_t(tiles(side, row_peer[j]), dz).astype(BF16)
            start(qs.at[d, j], qr.at[d, j], sq_s.at[d, j], sq_r.at[d, j], {"blk": where})

    g[0] = mm_t(y, d_message).reshape(g.shape[1:]).astype(BF16)
    g[1] = mm_t(smooth, cot_ref[...]).reshape(g.shape[1:]).astype(BF16)
    start(g.at[1 - c], grecv, sp, rp, {"blk": mate})
    upd_ref[...] = (x_ref[...].astype(F32) + mm(smooth, wu_ref[...])).astype(BF16)
    copy(grecv, grecv, sp, rp, {"blk": mate}).wait_recv()
    hbuf[...] = (g[c].astype(F32) + grecv[...].astype(F32)).astype(BF16)
    for i in range(1, ny):
        start(hbuf.at[y_peer[i]], yrecv.at[i - 1], sy.at[i - 1], ry.at[i - 1], {"blk": 2 * y_peer[i] + c})

    def summed(j):
        total = mm_t(tiles(1, row_peer[j]), ds[...].astype(BF16))
        for d, where in ((0, up), (1, down)):
            copy(qs.at[d, j], qr.at[d, j], sq_s.at[d, j], sq_r.at[d, j], {"blk": where}).wait_recv()
            total += qr[d, j].astype(F32)
        return total

    for j in range(1, nr):
        ss[j - 1] = summed(j).astype(BF16)
        start(ss.at[j - 1], sr.at[j - 1], st_s.at[j - 1], st_r.at[j - 1], {"rows": row_peer[j]})

    part = hbuf[yy].astype(F32)
    for i in range(1, ny):
        copy(yrecv.at[i - 1], yrecv.at[i - 1], sy.at[i - 1], ry.at[i - 1], {"blk": 2 * y_peer[i] + c}).wait_recv()
        part += yrecv[i - 1].astype(F32)
    h2[...] = part.astype(BF16)
    for j in range(1, nr):
        start(h2.at[row_peer[j]], zrecv.at[j - 1], sz.at[j - 1], rz.at[j - 1], {"rows": row_peer[j]})

    acc[...] = summed(0) + cot_ref[...].astype(F32)

    piece = h2[z].astype(F32)
    for j in range(1, nr):
        copy(zrecv.at[j - 1], zrecv.at[j - 1], sz.at[j - 1], rz.at[j - 1], {"rows": row_peer[j]}).wait_recv()
        piece += zrecv[j - 1].astype(F32)
    gout[c, yy, z] = piece.astype(BF16)
    for j in range(1, nr):
        start(gout.at[c, yy, z], gout.at[c, yy, z], sa.at[j - 1], ra.at[j - 1], {"rows": row_peer[j]})

    for j in range(1, nr):
        copy(ss.at[j - 1], sr.at[j - 1], st_s.at[j - 1], st_r.at[j - 1], {"rows": row_peer[j]}).wait_recv()
        acc[...] += sr[j - 1].astype(F32)
    df_ref[...] = acc[...].astype(BF16)

    for j in range(1, nr):
        place = gout.at[c, yy, row_peer[j]]
        copy(place, place, sa.at[j - 1], ra.at[j - 1], {"rows": row_peer[j]}).wait_recv()
    for i in range(1, ny):
        start(gout.at[c, yy], gout.at[c, yy], sb.at[i - 1], rb.at[i - 1], {"blk": 2 * y_peer[i] + c})
    start(gout.at[c, yy], gout.at[c, yy], sm.at[0], rm.at[0], {"blk": mate})
    for i in range(1, ny):
        place = gout.at[c, y_from[i]]
        copy(place, place, sb.at[i - 1], rb.at[i - 1], {"blk": 2 * y_peer[i] + c}).wait_recv()
        start(place, place, sm.at[i], rm.at[i], {"blk": mate})
    for i in range(ny):
        place = gout.at[1 - c, y_from[i]]
        copy(place, place, sm.at[i], rm.at[i], {"blk": mate}).wait_recv()
    for one in sends:
        one.wait_send()


def body(features, w_message, w_update, block_index, slot_count, edge_count, cotangent):
    nr = lax.axis_size("rows")
    nb = lax.axis_size("blk")
    ny = nb // 2
    lb = block_index.shape[0]
    rows, width = features.shape
    a, sq = dense(block_index, slot_count, edge_count, nb, nr)
    pr = width // (ny * nr)
    shard = (rows, width)
    dma = pltpu.SemaphoreType.DMA
    vmem = pl.BlockSpec(memory_space=pltpu.VMEM)
    n1 = nr - 1
    updated, d_features, grads = pl.pallas_call(
        functools.partial(layer_kernel, nb, nr, lb),
        out_shape=(
            jax.ShapeDtypeStruct(shard, BF16),
            jax.ShapeDtypeStruct(shard, BF16),
            jax.ShapeDtypeStruct((2, ny, nr, pr, width), BF16),
        ),
        in_specs=[vmem] * 6,
        out_specs=(vmem,) * 3,
        scratch_shapes=[
            pltpu.VMEM((3 * nr,) + shard, BF16),
            pltpu.VMEM((2, nr) + shard, BF16),
            pltpu.VMEM((2, nr) + shard, BF16),
            pltpu.VMEM((n1,) + shard, BF16),
            pltpu.VMEM((n1,) + shard, BF16),
            pltpu.VMEM(shard, F32),
            pltpu.VMEM(shard, F32),
            pltpu.VMEM((2, ny, nr, pr, width), BF16),
            pltpu.VMEM((ny, nr, pr, width), BF16),
            pltpu.VMEM((ny, nr, pr, width), BF16),
            pltpu.VMEM((ny - 1, nr, pr, width), BF16),
            pltpu.VMEM((nr, pr, width), BF16),
            pltpu.VMEM((n1, pr, width), BF16),
            dma((n1,)), dma((n1,)),
            dma((2, nr)), dma((2, nr)),
            dma((2, nr)), dma((2, nr)),
            dma((n1,)), dma((n1,)),
            dma, dma,
            dma((ny - 1,)), dma((ny - 1,)),
            dma((n1,)), dma((n1,)),
            dma((n1,)), dma((n1,)),
            dma((ny - 1,)), dma((ny - 1,)),
            dma((ny,)), dma((ny,)),
        ],
        compiler_params=pltpu.CompilerParams(
            collective_id=0, has_side_effects=True, vmem_limit_bytes=48 * 1024 * 1024
        ),
    )(a, sq, features, cotangent, w_message, w_update)
    scale = 1.0 / math.sqrt(rows * nb * nr)
    grad_message = grads[0].reshape(width, width).astype(F32) * scale
    grad_update = grads[1].reshape(width, width).astype(F32) * scale
    return (updated, d_features, grad_message, grad_update)


def solution(mesh):
    placed = (
        P(("parts", "blk", "rows"), None),
        P(),
        P(),
        P(("parts", "blk", "rows"), None),
        P(("parts", "blk", "rows")),
        P(("parts", "blk", "rows"), None, None, None),
        P(("parts", "blk", "rows"), None),
    )
    return jax.shard_map(
        body,
        mesh=mesh,
        in_specs=placed,
        out_specs=(
            P(("parts", "blk", "rows"), None),
            P(("parts", "blk", "rows"), None),
            P("parts", None),
            P("parts", None),
        ),
        check_vma=False,
    )
```

time: 342 us -> 105 us (0.31)
  waiting for transfers between devices: 223 us -> 0 us
  Pallas kernels: 0 us -> 96.4 us
  other arithmetic: 56.9 us -> 1.6 us
  matrix products: 23.6 us -> 0 us
  between operations: 13.9 us -> 0.7 us
  local copies, waits for them, and re-layouts: 18.4 us -> 5.23 us
  starting transfers between devices: 5.21 us -> 0 us
    psum x1 -> x0, waiting for transfers between devices: 96.6 us -> none  [body(): lax.psum((message_term, update_term), ('blk', 'rows'))]
    pallas_call x0 -> x2, Pallas kernels: none -> 96.4 us  [the longest x1 93.7 us: body(): pl.pallas_call(functools.partial(layer_kernel, nb, nr, lb), out_shape=(ja...]
    reduce_scatter x3 -> x0, waiting for transfers between devices: 51 us -> none  [the longest x1 28.6 us: body(): lax.psum_scatter(to_owner_after, 'rows', scatter_dimension=0, tiled=True)]
    ppermute x4 -> x0, waiting for transfers between devices: 46 us -> none  [from_behind(): lax.ppermute(array, axis, [(i, (i + by) % devices) for i in range(devices)])]
    scatter-add x1 -> x0, other arithmetic: 45.2 us -> none  [body(): partial_value.at[offsets.reshape(-1)]]
    all_gather x1 -> x0, waiting for transfers between devices: 29.7 us -> none  [body(): region_hidden = lax.all_gather(own_hidden, 'rows', axis=0, tiled=True)]
    dot_general x8 -> x0, matrix products: 23.6 us -> none  [the longest x1 8.64 us: body(): jnp.einsum('bsij,bid->bsjd', tiles_bf, d_message, preferred_element_type=...]
    gather x1 -> x0, local copies, waits for them, and re-layouts: 8.28 us -> none  [body(): sources = window[offsets]]
  transfers between devices with their start and end apart: 9 -> 0, of which waited for: 8 -> 0; matrix products, arithmetic and copies ran while one was open for 3% -> 0% of each run, Pallas kernels for 0% -> 0%
where the time goes in v1:
time: 105 us; the launch traced here: 104 us
  Pallas kernels  96.4 us (92%)
  local copies, waits for them, and re-layouts  5.23 us (5%)
  other arithmetic  1.6 us (2%)
    pallas_call x1, Pallas kernels, body(): pl.pallas_call(functools.partial(layer_kernel, nb, nr, lb), out_shape=(ja...  93.7 us
    unnamed x16, local copies, waits for them, and re-layouts  5.23 us
    pallas_call x1, Pallas kernels, dense(): pl.pallas_call(functools.partial(dense_kernel, nb, region_blocks), grid=(...  2.62 us

profile of v1, /device:TPU:0, one launch (start us, length us, event | category | flops | bytes accessed | tf_op | source)
XLA Modules:
  0.0 103.9 jit_solution(2495099280278497854)
XLA Ops:
  0.6 0.0 copy-start
  0.6 2.5 %copy-done = s32[2,40,128,128]{3,2,1,0:T(8,128)S(1)} copy-done((s32[2,40,128,128]{3,2,1,0:T(8,128)S(1)}, s32[2,40,128,128]{3,2,1,0:T(8,128)}, u32[]{:S(2)}) %copy-start) | copy-done | bytes 5242904
  3.1 0.0 copy-start.5
  3.1 0.7 copy-done.5
  3.8 0.0 copy-start.6
  3.8 0.7 copy-done.6
  4.5 0.0 copy-start.1
  4.5 0.0 copy-start.2
  4.5 0.0 copy-start.3
  4.5 0.0 copy-start.4
  4.5 2.6 %shard_map.102 = (bf16[24,256,128]{2,1,0:T(8,128)(2,1)S(1)}, bf16[256,128]{1,0:T(8,128)(2,1)S(1)}) custom-call(s32[2,40]{1,0:T(2,128)S(1)} %copy-done.5, s32[2]{0:T(128)S(1)} %copy-done.6, s32[2,40,128,128]{3,2,1,0:T(8,128)S(1)} %copy-done), custom_call_target="tpu_custom_call" | custom-call | tf_op jit(solution)/shard_map/pallas_call | solution.py:56
  7.1 0.0 copy-done.1
  7.1 0.0 copy-done.2
  7.1 0.0 copy-done.3
  7.1 0.0 copy-done.4
  7.1 93.7 %shard_map.103 = (bf16[256,512]{1,0:T(8,128)(2,1)S(1)}, bf16[256,512]{1,0:T(8,128)(2,1)S(1)}, bf16[2,2,4,64,512]{4,3,2,1,0:T(8,128)(2,1)S(1)}) custom-call(bf16[24,256,128]{2,1,0:T(8,128)(2,1)S(1)} %get-tuple-element.9.a_ref, bf16[256,128]{1,0:T(8,128)(2,1)S(1)} %get-tuple-element.10.sq_ref, bf16[256,512]{1,0:T(8,128)(2,1)S(1)} %copy-done.3, ...), custom_call_target="tpu_custom_call" | custom-call | tf_op jit(solution)/shard_map/pallas_call | solution.py:238
  100.9 1.6 %convert_multiply_fusion = (f32[1,2,4,64,512]{4,3,2,1,0:T(8,128)}, f32[1,2,4,64,512]{4,3,2,1,0:T(8,128)}) fusion(bf16[2,2,4,64,512]{4,3,2,1,0:T(8,128)(2,1)S(1)} %get-tuple-element.13), kind=kLoop, calls=%fused_computation | loop fusion | flops 1048576 | bytes 3145728 | tf_op jit(solution)/shard_map/mul | solution.py:278
  102.5 0.7 copy.13
  103.2 0.7 copy.14
Async XLA Ops:
  0.6 2.5 %copy-start = (s32[2,40,128,128]{3,2,1,0:T(8,128)S(1)}, s32[2,40,128,128]{3,2,1,0:T(8,128)}, u32[]{:S(2)}) copy-start(s32[2,40,128,128]{3,2,1,0:T(8,128)} %edge_ref.1) | copy-start | bytes 15728644
  3.1 0.7 copy-start.5
  3.8 0.7 copy-start.6
  4.5 2.6 %copy-start.1 = (bf16[512,512]{1,0:T(8,128)(2,1)S(1)}, bf16[512,512]{1,0:T(8,128)(2,1)}, u32[]{:S(2)}) copy-start(bf16[512,512]{1,0:T(8,128)(2,1)} %wm_ref.1) | copy-start | bytes 1572868
  4.5 2.6 %copy-start.2 = (bf16[512,512]{1,0:T(8,128)(2,1)S(1)}, bf16[512,512]{1,0:T(8,128)(2,1)}, u32[]{:S(2)}) copy-start(bf16[512,512]{1,0:T(8,128)(2,1)} %wu_ref.1) | copy-start | bytes 1572868
  4.5 2.7 %copy-start.3 = (bf16[256,512]{1,0:T(8,128)(2,1)S(1)}, bf16[256,512]{1,0:T(8,128)(2,1)}, u32[]{:S(2)}) copy-start(bf16[256,512]{1,0:T(8,128)(2,1)} %x_ref.1) | copy-start | bytes 786436
  4.5 2.7 %copy-start.4 = (bf16[256,512]{1,0:T(8,128)(2,1)S(1)}, bf16[256,512]{1,0:T(8,128)(2,1)}, u32[]{:S(2)}) copy-start(bf16[256,512]{1,0:T(8,128)(2,1)} %cot_ref.1) | copy-start | bytes 786436

commit v2 on v1

--- a/solution.py
+++ b/solution.py
@@ -12,15 +12,6 @@
 F32 = jnp.float32
 BF16 = jnp.bfloat16
 SLOT_STEP = 8
-
-
-def partner(z, j):
-    out, bit = z, 1
-    while bit <= j:
-        if j & bit:
-            out = out + bit * (1 - 2 * ((z // bit) % 2))
-        bit *= 2
-    return out
 
 
 def dense_kernel(nb, region_blocks, index_ref, count_ref, edge_ref, a_ref, sq_ref):
@@ -77,7 +68,7 @@
     nb, nr, lb,
     a_ref, sq_ref, x_ref, cot_ref, wm_ref, wu_ref,
     upd_ref, df_ref, gout,
-    xwin, qs, qr, ss, sr, acc, ds, g, grecv, hbuf, yrecv, h2, zrecv,
+    xwin, qs, qr, ss, sr, acc, ds, tot, dzb, smb, g, grecv, hbuf, yrecv, h2, zrecv,
     s1, r1, sf, rf, sq_s, sq_r, st_s, st_r,
     sp, rp, sy, ry, sz, rz, sa, ra, sb, rb, sm, rm,
 ):
@@ -88,7 +79,8 @@
     yy = r // 2
     mate = yy * 2 + (1 - c)
     up, down = lax.rem(r + 1, nb), lax.rem(r + nb - 1, nb)
-    row_peer = [partner(z, j) for j in range(nr)]
+    others = [lax.rem(z + j, nr) for j in range(nr)]
+    sources = [lax.rem(z + nr - j, nr) for j in range(nr)]
     y_peer = [lax.rem(yy + i, ny) for i in range(ny)]
     y_from = [lax.rem(yy + ny - i, ny) for i in range(ny)]
 
@@ -99,7 +91,7 @@
         )
 
     barrier = pltpu.get_barrier_semaphore()
-    peers = [{"rows": row_peer[j]} for j in range(1, nr)]
+    peers = [{"rows": others[j]} for j in range(1, nr)]
     peers += [{"blk": up}, {"blk": down}]
     peers += [{"blk": lax.rem(r + 2 * i, nb)} for i in range(1, ny)]
     for where in peers:
@@ -109,18 +101,50 @@
     sends = []
 
     def start(*args):
-        one = copy(*args)
-        one.start()
-        sends.append(one)
-
-    def forward(j):
-        src = x_ref if j == 0 else xwin.at[nr + row_peer[j]]
-        start(src, xwin.at[row_peer[j]], sf.at[0, j], rf.at[0, j], {"blk": up})
-        start(src, xwin.at[2 * nr + row_peer[j]], sf.at[1, j], rf.at[1, j], {"blk": down})
-
-    forward(0)
-    for j in range(1, nr):
-        start(x_ref, xwin.at[nr + z], s1.at[j - 1], r1.at[j - 1], {"rows": row_peer[j]})
+        start_when(None, lambda: args)
+
+    def start_when(when, make):
+        copy(*make()).start()
+        sends.append((when, make))
+
+    def guarded(when, run):
+        if when is None:
+            run()
+        else:
+            pl.when(when)(run)
+
+    def forward(src, shard, when=None):
+        for d, where in ((0, up), (1, down)):
+            start_when(
+                when,
+                lambda d=d, where=where: (
+                    src(), xwin.at[2 * d * nr + shard], sf.at[d, shard], rf.at[d, shard], {"blk": where}
+                ),
+            )
+
+    def along(way, t):
+        sign = 1 - 2 * way
+        there = z + sign
+        far = z + sign * t
+        near = z - sign
+        behind = z - sign * t
+        has_there = (there >= 0) & (there < nr)
+        has_far = (far >= 0) & (far < nr)
+        has_near = (near >= 0) & (near < nr)
+        has_behind = (behind >= 0) & (behind < nr)
+        return there, has_there, far, has_far, has_near, behind, has_behind
+
+    forward(lambda: x_ref, z)
+    for way in range(2):
+        there, has_there = along(way, 1)[:2]
+
+        def first(way=way, there=there, has_there=has_there):
+            start_when(
+                has_there,
+                lambda: (x_ref, xwin.at[nr + z], s1.at[way, 0], r1.at[way, 0], {"rows": there}),
+            )
+
+        pl.when(has_there)(first)
 
     def tiles(side, shard):
         first = (side * nr + shard) * lb
@@ -137,16 +161,42 @@
 
     ds[...] = mm_bt(cot_ref[...], wu_ref[...])
     acc[...] = mm(tiles(1, z), x_ref[...])
-    for j in range(1, nr):
-        slot = nr + row_peer[j]
-        copy(x_ref, xwin.at[slot], s1.at[j - 1], r1.at[j - 1], {"rows": row_peer[j]}).wait_recv()
-        forward(j)
-        acc[...] += mm(tiles(1, row_peer[j]), xwin[slot])
-    for j in range(nr):
-        for d, side, where in ((0, 0, up), (1, 2, down)):
-            slot = side * nr + row_peer[j]
-            copy(x_ref, xwin.at[slot], sf.at[d, j], rf.at[d, j], {"blk": where}).wait_recv()
-            acc[...] += mm(tiles(side, row_peer[j]), xwin[slot])
+    for t in range(1, nr):
+        for way in range(2):
+            there, has_there, far, has_far, has_near, behind, has_behind = along(way, t)
+
+            def arrive(way=way, t=t, behind=behind):
+                place = xwin.at[nr + behind]
+                copy(place, place, s1.at[way, t - 1], r1.at[way, t - 1], {"blk": up}).wait_recv()
+
+            def relay(way=way, t=t, there=there, behind=behind, when=has_there & has_behind):
+                start_when(
+                    when,
+                    lambda: (
+                        xwin.at[nr + behind], xwin.at[nr + behind], s1.at[way, t], r1.at[way, t], {"rows": there}
+                    ),
+                )
+
+            def use(way=way, t=t, behind=behind, has_there=has_there, has_behind=has_behind, relay=relay, arrive=arrive):
+                arrive()
+                if t < nr - 1:
+                    pl.when(has_there)(relay)
+                forward(lambda: xwin.at[nr + behind], behind, has_behind)
+                acc[...] += mm(tiles(1, behind), xwin[nr + behind])
+
+            pl.when(has_behind)(use)
+
+    def neighbour(shard):
+        for d, side in ((0, 0), (1, 2)):
+            slot = side * nr + shard
+            copy(xwin.at[slot], xwin.at[slot], sf.at[d, shard], rf.at[d, shard], {"blk": up}).wait_recv()
+            acc[...] += mm(tiles(side, shard), xwin[slot])
+
+    neighbour(z)
+    for t in range(1, nr):
+        for way in range(2):
+            behind, has_behind = along(way, t)[5:]
+            pl.when(has_behind)(functools.partial(neighbour, behind))
 
     inv = 1.0 / jnp.sqrt(1.0 + jnp.sum(sq_ref[...].astype(F32), axis=1, keepdims=True))
     y = acc[...].astype(BF16)
@@ -155,72 +205,116 @@
     smooth = (message * sig).astype(BF16)
     d_message = (ds[...] * sig * (1.0 + message * (1.0 - sig)) * inv).astype(BF16)
     dz = mm_bt(d_message, wm_ref[...]).astype(BF16)
-    ds[...] = dz.astype(F32)
-
-    order = list(range(1, nr)) + [0]
-    for j in order:
-        for d, side, where in ((0, 2, up), (1, 0, down)):
-            qs[d, j] = mm_t(tiles(side, row_peer[j]), dz).astype(BF16)
-            start(qs.at[d, j], qr.at[d, j], sq_s.at[d, j], sq_r.at[d, j], {"blk": where})
-
+    dzb[...] = dz
     g[0] = mm_t(y, d_message).reshape(g.shape[1:]).astype(BF16)
     g[1] = mm_t(smooth, cot_ref[...]).reshape(g.shape[1:]).astype(BF16)
+    smb[...] = smooth
     start(g.at[1 - c], grecv, sp, rp, {"blk": mate})
-    upd_ref[...] = (x_ref[...].astype(F32) + mm(smooth, wu_ref[...])).astype(BF16)
-    copy(grecv, grecv, sp, rp, {"blk": mate}).wait_recv()
-    hbuf[...] = (g[c].astype(F32) + grecv[...].astype(F32)).astype(BF16)
-    for i in range(1, ny):
-        start(hbuf.at[y_peer[i]], yrecv.at[i - 1], sy.at[i - 1], ry.at[i - 1], {"blk": 2 * y_peer[i] + c})
-
-    def summed(j):
-        total = mm_t(tiles(1, row_peer[j]), ds[...].astype(BF16))
-        for d, where in ((0, up), (1, down)):
-            copy(qs.at[d, j], qr.at[d, j], sq_s.at[d, j], sq_r.at[d, j], {"blk": where}).wait_recv()
-            total += qr[d, j].astype(F32)
-        return total
-
-    for j in range(1, nr):
-        ss[j - 1] = summed(j).astype(BF16)
-        start(ss.at[j - 1], sr.at[j - 1], st_s.at[j - 1], st_r.at[j - 1], {"rows": row_peer[j]})
-
-    part = hbuf[yy].astype(F32)
-    for i in range(1, ny):
-        copy(yrecv.at[i - 1], yrecv.at[i - 1], sy.at[i - 1], ry.at[i - 1], {"blk": 2 * y_peer[i] + c}).wait_recv()
-        part += yrecv[i - 1].astype(F32)
-    h2[...] = part.astype(BF16)
-    for j in range(1, nr):
-        start(h2.at[row_peer[j]], zrecv.at[j - 1], sz.at[j - 1], rz.at[j - 1], {"rows": row_peer[j]})
-
-    acc[...] = summed(0) + cot_ref[...].astype(F32)
-
-    piece = h2[z].astype(F32)
-    for j in range(1, nr):
-        copy(zrecv.at[j - 1], zrecv.at[j - 1], sz.at[j - 1], rz.at[j - 1], {"rows": row_peer[j]}).wait_recv()
-        piece += zrecv[j - 1].astype(F32)
-    gout[c, yy, z] = piece.astype(BF16)
-    for j in range(1, nr):
-        start(gout.at[c, yy, z], gout.at[c, yy, z], sa.at[j - 1], ra.at[j - 1], {"rows": row_peer[j]})
-
-    for j in range(1, nr):
-        copy(ss.at[j - 1], sr.at[j - 1], st_s.at[j - 1], st_r.at[j - 1], {"rows": row_peer[j]}).wait_recv()
-        acc[...] += sr[j - 1].astype(F32)
-    df_ref[...] = acc[...].astype(BF16)
-
-    for j in range(1, nr):
-        place = gout.at[c, yy, row_peer[j]]
-        copy(place, place, sa.at[j - 1], ra.at[j - 1], {"rows": row_peer[j]}).wait_recv()
-    for i in range(1, ny):
-        start(gout.at[c, yy], gout.at[c, yy], sb.at[i - 1], rb.at[i - 1], {"blk": 2 * y_peer[i] + c})
-    start(gout.at[c, yy], gout.at[c, yy], sm.at[0], rm.at[0], {"blk": mate})
+
+    def send_partials(shard, when=None):
+        for d, side, where in ((0, 2, up), (1, 0, down)):
+            qs[d, shard] = mm_t(tiles(side, shard), dzb[...]).astype(BF16)
+            start_when(
+                when,
+                lambda d=d, where=where: (
+                    qs.at[d, shard], qr.at[d, shard], sq_s.at[d, shard], sq_r.at[d, shard], {"blk": where}
+                ),
+            )
+
+    for t in range(nr - 1, 0, -1):
+        for way in range(2):
+            far, has_far = along(way, t)[2:4]
+            pl.when(has_far)(functools.partial(send_partials, far, has_far))
+    send_partials(z)
+    upd_ref[...] = (x_ref[...].astype(F32) + mm(smb[...], wu_ref[...])).astype(BF16)
+
+    def pair_sum():
+        copy(grecv, grecv, sp, rp, {"blk": mate}).wait_recv()
+        hbuf[...] = (g[c].astype(F32) + grecv[...].astype(F32)).astype(BF16)
+        for i in range(1, ny):
+            start(hbuf.at[y_peer[i]], yrecv.at[i - 1], sy.at[i - 1], ry.at[i - 1], {"blk": 2 * y_peer[i] + c})
+
+    def y_sum():
+        part = hbuf[yy].astype(F32)
+        for i in range(1, ny):
+            place = yrecv.at[i - 1]
+            copy(place, place, sy.at[i - 1], ry.at[i - 1], {"blk": mate}).wait_recv()
+            part += yrecv[i - 1].astype(F32)
+        h2[...] = part.astype(BF16)
+        for j in range(1, nr):
+            start(h2.at[others[j]], zrecv.at[j - 1], sz.at[j - 1], rz.at[j - 1], {"rows": others[j]})
+
+    def z_sum():
+        piece = h2[z].astype(F32)
+        for j in range(1, nr):
+            place = zrecv.at[j - 1]
+            copy(place, place, sz.at[j - 1], rz.at[j - 1], {"blk": mate}).wait_recv()
+            piece += zrecv[j - 1].astype(F32)
+        gout[c, yy, z] = piece.astype(BF16)
+        place = gout.at[c, yy, z]
+        for j in range(1, nr):
+            start(place, place, sa.at[j - 1], ra.at[j - 1], {"rows": others[j]})
+
+    def z_gather():
+        for j in range(1, nr):
+            place = gout.at[c, yy, sources[j]]
+            copy(place, place, sa.at[j - 1], ra.at[j - 1], {"blk": mate}).wait_recv()
+        place = gout.at[c, yy]
+        for i in range(1, ny):
+            start(place, place, sb.at[i - 1], rb.at[i - 1], {"blk": 2 * y_peer[i] + c})
+        start(place, place, sm.at[0], rm.at[0], {"blk": mate})
+
+    def summed(shard):
+        tot[...] = mm_t(tiles(1, shard), dzb[...])
+        for d in range(2):
+            place = qr.at[d, shard]
+            copy(place, place, sq_s.at[d, shard], sq_r.at[d, shard], {"blk": up}).wait_recv()
+            tot[...] += qr[d, shard].astype(F32)
+
+    def add_arrived(way, t):
+        place = sr.at[way, t]
+        copy(place, place, st_s.at[way, t], st_r.at[way, t], {"blk": up}).wait_recv()
+        tot[...] += sr[way, t].astype(F32)
+
+    pair_sum()
+    between = [y_sum, z_sum, z_gather]
+    for t in range(nr - 1, 0, -1):
+        for way in range(2):
+            there, has_there, far, has_far, has_near, behind, has_behind = along(way, t)
+
+            def pass_on(way=way, t=t, there=there, far=far, has_far=has_far, has_near=has_near):
+                summed(far)
+                if t < nr - 1:
+                    pl.when(has_near)(functools.partial(add_arrived, way, t))
+                ss[way, t - 1] = tot[...].astype(BF16)
+                start_when(
+                    has_far,
+                    lambda: (
+                        ss.at[way, t - 1], sr.at[way, t - 1], st_s.at[way, t - 1], st_r.at[way, t - 1],
+                        {"rows": there},
+                    ),
+                )
+
+            pl.when(has_far)(pass_on)
+        if between:
+            between.pop(0)()
+    for run in between:
+        run()
+    summed(z)
+    for way in range(2):
+        has_near = along(way, 1)[4]
+        pl.when(has_near)(functools.partial(add_arrived, way, 0))
+    df_ref[...] = (tot[...] + cot_ref[...].astype(F32)).astype(BF16)
+
     for i in range(1, ny):
         place = gout.at[c, y_from[i]]
-        copy(place, place, sb.at[i - 1], rb.at[i - 1], {"blk": 2 * y_peer[i] + c}).wait_recv()
+        copy(place, place, sb.at[i - 1], rb.at[i - 1], {"blk": mate}).wait_recv()
         start(place, place, sm.at[i], rm.at[i], {"blk": mate})
     for i in range(ny):
         place = gout.at[1 - c, y_from[i]]
         copy(place, place, sm.at[i], rm.at[i], {"blk": mate}).wait_recv()
-    for one in sends:
-        one.wait_send()
+    for when, make in sends:
+        guarded(when, lambda make=make: copy(*make()).wait_send())
 
 
 def body(features, w_message, w_update, block_index, slot_count, edge_count, cotangent):
@@ -248,20 +342,23 @@
             pltpu.VMEM((3 * nr,) + shard, BF16),
             pltpu.VMEM((2, nr) + shard, BF16),
             pltpu.VMEM((2, nr) + shard, BF16),
-            pltpu.VMEM((n1,) + shard, BF16),
-            pltpu.VMEM((n1,) + shard, BF16),
+            pltpu.VMEM((2, n1) + shard, BF16),
+            pltpu.VMEM((2, n1) + shard, BF16),
             pltpu.VMEM(shard, F32),
             pltpu.VMEM(shard, F32),
+            pltpu.VMEM(shard, F32),
+            pltpu.VMEM(shard, BF16),
+            pltpu.VMEM(shard, BF16),
             pltpu.VMEM((2, ny, nr, pr, width), BF16),
             pltpu.VMEM((ny, nr, pr, width), BF16),
             pltpu.VMEM((ny, nr, pr, width), BF16),
             pltpu.VMEM((ny - 1, nr, pr, width), BF16),
             pltpu.VMEM((nr, pr, width), BF16),
             pltpu.VMEM((n1, pr, width), BF16),
-            dma((n1,)), dma((n1,)),
+            dma((2, n1)), dma((2, n1)),
             dma((2, nr)), dma((2, nr)),
             dma((2, nr)), dma((2, nr)),
-            dma((n1,)), dma((n1,)),
+            dma((2, n1)), dma((2, n1)),
             dma, dma,
             dma((ny - 1,)), dma((ny - 1,)),
             dma((n1,)), dma((n1,)),

time: 105 us -> 98.2 us (0.935)
  the two profiles are of different devices: /device:TPU:0 before, /device:TPU:11 now
where the time goes in v2:
time: 98.2 us; the launch traced here: 98 us
  Pallas kernels  90.4 us (92%)
  local copies, waits for them, and re-layouts  5.23 us (5%)
  other arithmetic  1.6 us (2%)
    pallas_call x1, Pallas kernels, body(): pl.pallas_call(functools.partial(layer_kernel, nb, nr, lb), out_shape=(ja...  88 us
    unnamed x16, local copies, waits for them, and re-layouts  5.23 us
    pallas_call x1, Pallas kernels, dense(): pl.pallas_call(functools.partial(dense_kernel, nb, region_blocks), grid=(...  2.38 us

profile of v2, /device:TPU:11, one launch (start us, length us, event | category | flops | bytes accessed | tf_op | source)
XLA Modules:
  0.0 98.0 jit_solution(14788056303644479720)
XLA Ops:
  0.6 0.0 copy-start
  0.6 2.5 %copy-done = s32[2,40,128,128]{3,2,1,0:T(8,128)S(1)} copy-done((s32[2,40,128,128]{3,2,1,0:T(8,128)S(1)}, s32[2,40,128,128]{3,2,1,0:T(8,128)}, u32[]{:S(2)}) %copy-start) | copy-done | bytes 5242904
  3.1 0.0 copy-start.5
  3.1 0.7 copy-done.5
  3.8 0.0 copy-start.6
  3.8 0.7 copy-done.6
  4.5 0.0 copy-start.1
  4.5 0.0 copy-start.2
  4.5 0.0 copy-start.3
  4.5 0.0 copy-start.4
  4.5 2.4 %shard_map.102 = (bf16[24,256,128]{2,1,0:T(8,128)(2,1)S(1)}, bf16[256,128]{1,0:T(8,128)(2,1)S(1)}) custom-call(s32[2,40]{1,0:T(2,128)S(1)} %copy-done.5, s32[2]{0:T(128)S(1)} %copy-done.6, s32[2,40,128,128]{3,2,1,0:T(8,128)S(1)} %copy-done), custom_call_target="tpu_custom_call" | custom-call | tf_op jit(solution)/shard_map/pallas_call | solution.py:47
  6.9 0.0 copy-done.1
  6.9 0.0 copy-done.2
  6.9 0.0 copy-done.3
  6.9 0.0 copy-done.4
  6.9 88.0 %shard_map.103 = (bf16[256,512]{1,0:T(8,128)(2,1)S(1)}, bf16[256,512]{1,0:T(8,128)(2,1)S(1)}, bf16[2,2,4,64,512]{4,3,2,1,0:T(8,128)(2,1)S(1)}) custom-call(bf16[24,256,128]{2,1,0:T(8,128)(2,1)S(1)} %get-tuple-element.9.a_ref, bf16[256,128]{1,0:T(8,128)(2,1)S(1)} %get-tuple-element.10.sq_ref, bf16[256,512]{1,0:T(8,128)(2,1)S(1)} %copy-done.3, ...), custom_call_target="tpu_custom_call" | custom-call | tf_op jit(solution)/shard_map/pallas_call | solution.py:332
  95.0 1.6 %convert_multiply_fusion = (f32[1,2,4,64,512]{4,3,2,1,0:T(8,128)}, f32[1,2,4,64,512]{4,3,2,1,0:T(8,128)}) fusion(bf16[2,2,4,64,512]{4,3,2,1,0:T(8,128)(2,1)S(1)} %get-tuple-element.13), kind=kLoop, calls=%fused_computation | loop fusion | flops 1048576 | bytes 3145728 | tf_op jit(solution)/shard_map/mul | solution.py:375
  96.5 0.7 copy.13
  97.3 0.7 copy.14
Async XLA Ops:
  0.6 2.5 %copy-start = (s32[2,40,128,128]{3,2,1,0:T(8,128)S(1)}, s32[2,40,128,128]{3,2,1,0:T(8,128)}, u32[]{:S(2)}) copy-start(s32[2,40,128,128]{3,2,1,0:T(8,128)} %edge_ref.1) | copy-start | bytes 15728644
  3.1 0.7 copy-start.5
  3.8 0.7 copy-start.6
  4.5 2.4 %copy-start.1 = (bf16[512,512]{1,0:T(8,128)(2,1)S(1)}, bf16[512,512]{1,0:T(8,128)(2,1)}, u32[]{:S(2)}) copy-start(bf16[512,512]{1,0:T(8,128)(2,1)} %wm_ref.1) | copy-start | bytes 1572868
  4.5 2.4 %copy-start.2 = (bf16[512,512]{1,0:T(8,128)(2,1)S(1)}, bf16[512,512]{1,0:T(8,128)(2,1)}, u32[]{:S(2)}) copy-start(bf16[512,512]{1,0:T(8,128)(2,1)} %wu_ref.1) | copy-start | bytes 1572868
  4.5 2.4 %copy-start.3 = (bf16[256,512]{1,0:T(8,128)(2,1)S(1)}, bf16[256,512]{1,0:T(8,128)(2,1)}, u32[]{:S(2)}) copy-start(bf16[256,512]{1,0:T(8,128)(2,1)} %x_ref.1) | copy-start | bytes 786436
  4.5 2.4 %copy-start.4 = (bf16[256,512]{1,0:T(8,128)(2,1)S(1)}, bf16[256,512]{1,0:T(8,128)(2,1)}, u32[]{:S(2)}) copy-start(bf16[256,512]{1,0:T(8,128)(2,1)} %cot_ref.1) | copy-start | bytes 786436

commit v3 on v2

--- a/solution.py
+++ b/solution.py
@@ -113,12 +113,12 @@
         else:
             pl.when(when)(run)
 
-    def forward(src, shard, when=None):
+    def forward(src, shard, h, when=None):
         for d, where in ((0, up), (1, down)):
             start_when(
                 when,
                 lambda d=d, where=where: (
-                    src(), xwin.at[2 * d * nr + shard], sf.at[d, shard], rf.at[d, shard], {"blk": where}
+                    src(), xwin.at[2 * d * nr + shard, h], sf.at[d, shard, h], rf.at[d, shard, h], {"blk": where}
                 ),
             )
 
@@ -134,17 +134,21 @@
         has_behind = (behind >= 0) & (behind < nr)
         return there, has_there, far, has_far, has_near, behind, has_behind
 
-    forward(lambda: x_ref, z)
-    for way in range(2):
-        there, has_there = along(way, 1)[:2]
-
-        def first(way=way, there=there, has_there=has_there):
-            start_when(
-                has_there,
-                lambda: (x_ref, xwin.at[nr + z], s1.at[way, 0], r1.at[way, 0], {"rows": there}),
-            )
-
-        pl.when(has_there)(first)
+    for h in range(lb):
+        forward(lambda h=h: x_ref.at[h], z, h)
+        for way in range(2):
+            there, has_there = along(way, 1)[:2]
+
+            def first(way=way, there=there, has_there=has_there, h=h):
+                start_when(
+                    has_there,
+                    lambda: (x_ref.at[h], xwin.at[nr + z, h], s1.at[way, 0, h], r1.at[way, 0, h], {"rows": there}),
+                )
+
+            pl.when(has_there)(first)
+
+    def flat(value):
+        return value.reshape(value.shape[0] * value.shape[1], value.shape[2])
 
     def tiles(side, shard):
         first = (side * nr + shard) * lb
@@ -160,37 +164,38 @@
         return lax.dot_general(a, b, (((1,), (1,)), ((), ())), preferred_element_type=F32)
 
     ds[...] = mm_bt(cot_ref[...], wu_ref[...])
-    acc[...] = mm(tiles(1, z), x_ref[...])
+    acc[...] = mm(tiles(1, z), flat(x_ref[...]))
     for t in range(1, nr):
         for way in range(2):
             there, has_there, far, has_far, has_near, behind, has_behind = along(way, t)
 
-            def arrive(way=way, t=t, behind=behind):
-                place = xwin.at[nr + behind]
-                copy(place, place, s1.at[way, t - 1], r1.at[way, t - 1], {"blk": up}).wait_recv()
-
-            def relay(way=way, t=t, there=there, behind=behind, when=has_there & has_behind):
+            def relay(way=way, t=t, there=there, behind=behind, when=has_there & has_behind, h=0):
                 start_when(
                     when,
                     lambda: (
-                        xwin.at[nr + behind], xwin.at[nr + behind], s1.at[way, t], r1.at[way, t], {"rows": there}
+                        xwin.at[nr + behind, h], xwin.at[nr + behind, h],
+                        s1.at[way, t, h], r1.at[way, t, h], {"rows": there},
                     ),
                 )
 
-            def use(way=way, t=t, behind=behind, has_there=has_there, has_behind=has_behind, relay=relay, arrive=arrive):
-                arrive()
-                if t < nr - 1:
-                    pl.when(has_there)(relay)
-                forward(lambda: xwin.at[nr + behind], behind, has_behind)
-                acc[...] += mm(tiles(1, behind), xwin[nr + behind])
+            def use(way=way, t=t, behind=behind, has_there=has_there, has_behind=has_behind, relay=relay):
+                for h in range(lb):
+                    place = xwin.at[nr + behind, h]
+                    copy(place, place, s1.at[way, t - 1, h], r1.at[way, t - 1, h], {"blk": up}).wait_recv()
+                    if t < nr - 1:
+                        pl.when(has_there)(functools.partial(relay, h=h))
+                    forward(lambda h=h: xwin.at[nr + behind, h], behind, h, has_behind)
+                acc[...] += mm(tiles(1, behind), flat(xwin[nr + behind]))
 
             pl.when(has_behind)(use)
 
     def neighbour(shard):
         for d, side in ((0, 0), (1, 2)):
             slot = side * nr + shard
-            copy(xwin.at[slot], xwin.at[slot], sf.at[d, shard], rf.at[d, shard], {"blk": up}).wait_recv()
-            acc[...] += mm(tiles(side, shard), xwin[slot])
+            for h in range(lb):
+                place = xwin.at[slot, h]
+                copy(place, place, sf.at[d, shard, h], rf.at[d, shard, h], {"blk": up}).wait_recv()
+            acc[...] += mm(tiles(side, shard), flat(xwin[slot]))
 
     neighbour(z)
     for t in range(1, nr):
@@ -213,20 +218,23 @@
 
     def send_partials(shard, when=None):
         for d, side, where in ((0, 2, up), (1, 0, down)):
-            qs[d, shard] = mm_t(tiles(side, shard), dzb[...]).astype(BF16)
-            start_when(
-                when,
-                lambda d=d, where=where: (
-                    qs.at[d, shard], qr.at[d, shard], sq_s.at[d, shard], sq_r.at[d, shard], {"blk": where}
-                ),
-            )
-
-    for t in range(nr - 1, 0, -1):
+            qs[d, shard] = mm_t(tiles(side, shard), dzb[...]).reshape(x_ref.shape).astype(BF16)
+            for h in range(lb):
+                start_when(
+                    when,
+                    lambda d=d, where=where, h=h: (
+                        qs.at[d, shard, h], qr.at[d, shard, h],
+                        sq_s.at[d, shard, h], sq_r.at[d, shard, h], {"blk": where},
+                    ),
+                )
+
+    def send_step(t):
+        if t == 0:
+            send_partials(z)
+            return
         for way in range(2):
             far, has_far = along(way, t)[2:4]
             pl.when(has_far)(functools.partial(send_partials, far, has_far))
-    send_partials(z)
-    upd_ref[...] = (x_ref[...].astype(F32) + mm(smb[...], wu_ref[...])).astype(BF16)
 
     def pair_sum():
         copy(grecv, grecv, sp, rp, {"blk": mate}).wait_recv()
@@ -264,47 +272,58 @@
             start(place, place, sb.at[i - 1], rb.at[i - 1], {"blk": 2 * y_peer[i] + c})
         start(place, place, sm.at[0], rm.at[0], {"blk": mate})
 
-    def summed(shard):
-        tot[...] = mm_t(tiles(1, shard), dzb[...])
+    def own_part(shard):
+        tot[...] = mm_t(tiles(1, shard), dzb[...]).reshape(tot.shape)
+
+    def add_partials(shard, h):
         for d in range(2):
-            place = qr.at[d, shard]
-            copy(place, place, sq_s.at[d, shard], sq_r.at[d, shard], {"blk": up}).wait_recv()
-            tot[...] += qr[d, shard].astype(F32)
-
-    def add_arrived(way, t):
-        place = sr.at[way, t]
-        copy(place, place, st_s.at[way, t], st_r.at[way, t], {"blk": up}).wait_recv()
-        tot[...] += sr[way, t].astype(F32)
-
+            place = qr.at[d, shard, h]
+            copy(place, place, sq_s.at[d, shard, h], sq_r.at[d, shard, h], {"blk": up}).wait_recv()
+            tot[h] += qr[d, shard, h].astype(F32)
+
+    def add_arrived(way, t, h):
+        place = sr.at[way, t, h]
+        copy(place, place, st_s.at[way, t, h], st_r.at[way, t, h], {"blk": up}).wait_recv()
+        tot[h] += sr[way, t, h].astype(F32)
+
+    send_step(nr - 1)
     pair_sum()
+    send_step(nr - 2)
+    upd_ref[...] = (flat(x_ref[...]).astype(F32) + mm(smb[...], wu_ref[...])).astype(BF16)
     between = [y_sum, z_sum, z_gather]
     for t in range(nr - 1, 0, -1):
+        if t >= 2:
+            send_step(t - 2)
         for way in range(2):
             there, has_there, far, has_far, has_near, behind, has_behind = along(way, t)
 
             def pass_on(way=way, t=t, there=there, far=far, has_far=has_far, has_near=has_near):
-                summed(far)
-                if t < nr - 1:
-                    pl.when(has_near)(functools.partial(add_arrived, way, t))
-                ss[way, t - 1] = tot[...].astype(BF16)
-                start_when(
-                    has_far,
-                    lambda: (
-                        ss.at[way, t - 1], sr.at[way, t - 1], st_s.at[way, t - 1], st_r.at[way, t - 1],
-                        {"rows": there},
-                    ),
-                )
+                own_part(far)
+                for h in range(lb):
+                    add_partials(far, h)
+                    if t < nr - 1:
+                        pl.when(has_near)(functools.partial(add_arrived, way, t, h))
+                    ss[way, t - 1, h] = tot[h].astype(BF16)
+                    start_when(
+                        has_far,
+                        lambda h=h: (
+                            ss.at[way, t - 1, h], sr.at[way, t - 1, h],
+                            st_s.at[way, t - 1, h], st_r.at[way, t - 1, h], {"rows": there},
+                        ),
+                    )
 
             pl.when(has_far)(pass_on)
         if between:
             between.pop(0)()
     for run in between:
         run()
-    summed(z)
-    for way in range(2):
-        has_near = along(way, 1)[4]
-        pl.when(has_near)(functools.partial(add_arrived, way, 0))
-    df_ref[...] = (tot[...] + cot_ref[...].astype(F32)).astype(BF16)
+    own_part(z)
+    for h in range(lb):
+        add_partials(z, h)
+        for way in range(2):
+            has_near = along(way, 1)[4]
+            pl.when(has_near)(functools.partial(add_arrived, way, 0, h))
+    df_ref[...] = (flat(tot[...]) + cot_ref[...].astype(F32)).astype(BF16)
 
     for i in range(1, ny):
         place = gout.at[c, y_from[i]]
@@ -326,6 +345,7 @@
     a, sq = dense(block_index, slot_count, edge_count, nb, nr)
     pr = width // (ny * nr)
     shard = (rows, width)
+    halves = (lb, rows // lb, width)
     dma = pltpu.SemaphoreType.DMA
     vmem = pl.BlockSpec(memory_space=pltpu.VMEM)
     n1 = nr - 1
@@ -339,14 +359,14 @@
         in_specs=[vmem] * 6,
         out_specs=(vmem,) * 3,
         scratch_shapes=[
-            pltpu.VMEM((3 * nr,) + shard, BF16),
-            pltpu.VMEM((2, nr) + shard, BF16),
-            pltpu.VMEM((2, nr) + shard, BF16),
-            pltpu.VMEM((2, n1) + shard, BF16),
-            pltpu.VMEM((2, n1) + shard, BF16),
+            pltpu.VMEM((3 * nr,) + halves, BF16),
+            pltpu.VMEM((2, nr) + halves, BF16),
+            pltpu.VMEM((2, nr) + halves, BF16),
+            pltpu.VMEM((2, n1) + halves, BF16),
+            pltpu.VMEM((2, n1) + halves, BF16),
             pltpu.VMEM(shard, F32),
             pltpu.VMEM(shard, F32),
-            pltpu.VMEM(shard, F32),
+            pltpu.VMEM(halves, F32),
             pltpu.VMEM(shard, BF16),
             pltpu.VMEM(shard, BF16),
             pltpu.VMEM((2, ny, nr, pr, width), BF16),
@@ -355,10 +375,10 @@
             pltpu.VMEM((ny - 1, nr, pr, width), BF16),
             pltpu.VMEM((nr, pr, width), BF16),
             pltpu.VMEM((n1, pr, width), BF16),
-            dma((2, n1)), dma((2, n1)),
-            dma((2, nr)), dma((2, nr)),
-            dma((2, nr)), dma((2, nr)),
-            dma((2, n1)), dma((2, n1)),
+            dma((2, n1, lb)), dma((2, n1, lb)),
+            dma((2, nr, lb)), dma((2, nr, lb)),
+            dma((2, nr, lb)), dma((2, nr, lb)),
+            dma((2, n1, lb)), dma((2, n1, lb)),
             dma, dma,
             dma((ny - 1,)), dma((ny - 1,)),
             dma((n1,)), dma((n1,)),
@@ -369,7 +389,7 @@
         compiler_params=pltpu.CompilerParams(
             collective_id=0, has_side_effects=True, vmem_limit_bytes=48 * 1024 * 1024
         ),
-    )(a, sq, features, cotangent, w_message, w_update)
+    )(a, sq, features.reshape(halves), cotangent, w_message, w_update)
     scale = 1.0 / math.sqrt(rows * nb * nr)
     grad_message = grads[0].reshape(width, width).astype(F32) * scale
     grad_update = grads[1].reshape(width, width).astype(F32) * scale

time: 98.2 us -> 78.3 us (0.80)
  the two profiles are of different devices: /device:TPU:11 before, /device:TPU:0 now
where the time goes in v3:
time: 78.3 us; the launch traced here: 77.2 us
  Pallas kernels  69.7 us (89%)
  local copies, waits for them, and re-layouts  5.23 us (7%)
  other arithmetic  1.6 us (2%)
    pallas_call x1, Pallas kernels, body(): pl.pallas_call(functools.partial(layer_kernel, nb, nr, lb), out_shape=(ja...  67.3 us
    unnamed x16, local copies, waits for them, and re-layouts  5.23 us
    pallas_call x1, Pallas kernels, dense(): pl.pallas_call(functools.partial(dense_kernel, nb, region_blocks), grid=(...  2.34 us
    mul x1, other arithmetic, body(): grad_update = grads[1].reshape(width, width).astype(F32) * scale  1.6 us

profile of v3, /device:TPU:0, one launch (start us, length us, event | category | flops | bytes accessed | tf_op | source)
XLA Modules:
  0.0 77.2 jit_solution(16695902951625154031)
XLA Ops:
  0.6 0.0 copy-start
  0.6 2.5 %copy-done = s32[2,40,128,128]{3,2,1,0:T(8,128)S(1)} copy-done((s32[2,40,128,128]{3,2,1,0:T(8,128)S(1)}, s32[2,40,128,128]{3,2,1,0:T(8,128)}, u32[]{:S(2)}) %copy-start) | copy-done | bytes 5242904
  3.1 0.0 copy-start.5
  3.1 0.7 copy-done.5
  3.8 0.0 copy-start.6
  3.8 0.7 copy-done.6
  4.5 0.0 copy-start.1
  4.5 0.0 copy-start.2
  4.5 0.0 copy-start.3
  4.5 0.0 copy-start.4
  4.5 2.3 %shard_map.102 = (bf16[24,256,128]{2,1,0:T(8,128)(2,1)S(1)}, bf16[256,128]{1,0:T(8,128)(2,1)S(1)}) custom-call(s32[2,40]{1,0:T(2,128)S(1)} %copy-done.5, s32[2]{0:T(128)S(1)} %copy-done.6, s32[2,40,128,128]{3,2,1,0:T(8,128)S(1)} %copy-done), custom_call_target="tpu_custom_call" | custom-call | tf_op jit(solution)/shard_map/pallas_call | solution.py:47
  6.8 0.0 copy-done.1
  6.8 0.0 copy-done.2
  6.8 0.0 copy-done.3
  6.8 0.0 copy-done.4
  6.9 67.3 %shard_map.103 = (bf16[256,512]{1,0:T(8,128)(2,1)S(1)}, bf16[256,512]{1,0:T(8,128)(2,1)S(1)}, bf16[2,2,4,64,512]{4,3,2,1,0:T(8,128)(2,1)S(1)}) custom-call(bf16[24,256,128]{2,1,0:T(8,128)(2,1)S(1)} %get-tuple-element.9.a_ref, bf16[256,128]{1,0:T(8,128)(2,1)S(1)} %get-tuple-element.10.sq_ref, bf16[2,128,512]{2,1,0:T(8,128)(2,1)S(1)} %bitcast.3, ...), custom_call_target="tpu_custom_call" | custom-call | tf_op jit(solution)/shard_map/pallas_call | solution.py:352
  74.2 1.6 %convert_multiply_fusion = (f32[1,2,4,64,512]{4,3,2,1,0:T(8,128)}, f32[1,2,4,64,512]{4,3,2,1,0:T(8,128)}) fusion(bf16[2,2,4,64,512]{4,3,2,1,0:T(8,128)(2,1)S(1)} %get-tuple-element.13), kind=kLoop, calls=%fused_computation | loop fusion | flops 1048576 | bytes 3145728 | tf_op jit(solution)/shard_map/mul | solution.py:395
  75.8 0.7 copy.13
  76.5 0.7 copy.14
Async XLA Ops:
  0.6 2.5 %copy-start = (s32[2,40,128,128]{3,2,1,0:T(8,128)S(1)}, s32[2,40,128,128]{3,2,1,0:T(8,128)}, u32[]{:S(2)}) copy-start(s32[2,40,128,128]{3,2,1,0:T(8,128)} %edge_ref.1) | copy-start | bytes 15728644
  3.1 0.7 copy-start.5
  3.8 0.7 copy-start.6
  4.5 2.4 %copy-start.1 = (bf16[512,512]{1,0:T(8,128)(2,1)S(1)}, bf16[512,512]{1,0:T(8,128)(2,1)}, u32[]{:S(2)}) copy-start(bf16[512,512]{1,0:T(8,128)(2,1)} %wm_ref.1) | copy-start | bytes 1572868
  4.5 2.4 %copy-start.2 = (bf16[512,512]{1,0:T(8,128)(2,1)S(1)}, bf16[512,512]{1,0:T(8,128)(2,1)}, u32[]{:S(2)}) copy-start(bf16[512,512]{1,0:T(8,128)(2,1)} %wu_ref.1) | copy-start | bytes 1572868
  4.5 2.4 %copy-start.3 = (bf16[256,512]{1,0:T(8,128)(2,1)S(1)}, bf16[256,512]{1,0:T(8,128)(2,1)}, u32[]{:S(2)}) copy-start(bf16[256,512]{1,0:T(8,128)(2,1)} %param.7) | copy-start | bytes 786436
  4.5 2.4 %copy-start.4 = (bf16[256,512]{1,0:T(8,128)(2,1)S(1)}, bf16[256,512]{1,0:T(8,128)(2,1)}, u32[]{:S(2)}) copy-start(bf16[256,512]{1,0:T(8,128)(2,1)} %cot_ref.1) | copy-start | bytes 786436

commit v4 on v3

--- a/solution.py
+++ b/solution.py
@@ -11,7 +11,7 @@
 MESH = pl.DeviceIdType.MESH
 F32 = jnp.float32
 BF16 = jnp.bfloat16
-SLOT_STEP = 8
+SLOT_STEP = 40
 
 
 def dense_kernel(nb, region_blocks, index_ref, count_ref, edge_ref, a_ref, sq_ref):

time: 78.3 us -> 77.6 us (level)
  no operation moved by 1% of the time
where the time goes in v4:
time: 77.6 us; the launch traced here: 76.5 us
  Pallas kernels  69 us (89%)
  local copies, waits for them, and re-layouts  5.23 us (7%)
  other arithmetic  1.6 us (2%)
    pallas_call x1, Pallas kernels, body(): pl.pallas_call(functools.partial(layer_kernel, nb, nr, lb), out_shape=(ja...  66.8 us
    unnamed x16, local copies, waits for them, and re-layouts  5.23 us
    pallas_call x1, Pallas kernels, dense(): pl.pallas_call(functools.partial(dense_kernel, nb, region_blocks), grid=(...  2.11 us
    mul x1, other arithmetic, body(): grad_update = grads[1].reshape(width, width).astype(F32) * scale  1.6 us

profile of v4, /device:TPU:0, one launch (start us, length us, event | category | flops | bytes accessed | tf_op | source)
XLA Modules:
  0.0 76.5 jit_solution(13069667088023622817)
XLA Ops:
  0.6 0.0 copy-start
  0.6 2.5 %copy-done = s32[2,40,128,128]{3,2,1,0:T(8,128)S(1)} copy-done((s32[2,40,128,128]{3,2,1,0:T(8,128)S(1)}, s32[2,40,128,128]{3,2,1,0:T(8,128)}, u32[]{:S(2)}) %copy-start) | copy-done | bytes 5242904
  3.1 0.0 copy-start.5
  3.1 0.7 copy-done.5
  3.8 0.0 copy-start.6
  3.8 0.7 copy-done.6
  4.5 0.0 copy-start.1
  4.5 0.0 copy-start.2
  4.5 0.0 copy-start.3
  4.5 0.0 copy-start.4
  4.5 2.1 %shard_map.102 = (bf16[24,256,128]{2,1,0:T(8,128)(2,1)S(1)}, bf16[256,128]{1,0:T(8,128)(2,1)S(1)}) custom-call(s32[2,40]{1,0:T(2,128)S(1)} %copy-done.5, s32[2]{0:T(128)S(1)} %copy-done.6, s32[2,40,128,128]{3,2,1,0:T(8,128)S(1)} %copy-done), custom_call_target="tpu_custom_call" | custom-call | tf_op jit(solution)/shard_map/pallas_call | solution.py:47
  6.6 0.0 copy-done.1
  6.6 0.0 copy-done.2
  6.6 0.0 copy-done.3
  6.6 0.0 copy-done.4
  6.6 66.8 %shard_map.103 = (bf16[256,512]{1,0:T(8,128)(2,1)S(1)}, bf16[256,512]{1,0:T(8,128)(2,1)S(1)}, bf16[2,2,4,64,512]{4,3,2,1,0:T(8,128)(2,1)S(1)}) custom-call(bf16[24,256,128]{2,1,0:T(8,128)(2,1)S(1)} %get-tuple-element.9.a_ref, bf16[256,128]{1,0:T(8,128)(2,1)S(1)} %get-tuple-element.10.sq_ref, bf16[2,128,512]{2,1,0:T(8,128)(2,1)S(1)} %bitcast.3, ...), custom_call_target="tpu_custom_call" | custom-call | tf_op jit(solution)/shard_map/pallas_call | solution.py:352
  73.5 1.6 %convert_multiply_fusion = (f32[1,2,4,64,512]{4,3,2,1,0:T(8,128)}, f32[1,2,4,64,512]{4,3,2,1,0:T(8,128)}) fusion(bf16[2,2,4,64,512]{4,3,2,1,0:T(8,128)(2,1)S(1)} %get-tuple-element.13), kind=kLoop, calls=%fused_computation | loop fusion | flops 1048576 | bytes 3145728 | tf_op jit(solution)/shard_map/mul | solution.py:395
  75.1 0.7 copy.13
  75.8 0.7 copy.14
Async XLA Ops:
  0.6 2.5 %copy-start = (s32[2,40,128,128]{3,2,1,0:T(8,128)S(1)}, s32[2,40,128,128]{3,2,1,0:T(8,128)}, u32[]{:S(2)}) copy-start(s32[2,40,128,128]{3,2,1,0:T(8,128)} %edge_ref.1) | copy-start | bytes 15728644
  3.1 0.7 copy-start.5
  3.8 0.7 copy-start.6
  4.5 2.1 %copy-start.1 = (bf16[512,512]{1,0:T(8,128)(2,1)S(1)}, bf16[512,512]{1,0:T(8,128)(2,1)}, u32[]{:S(2)}) copy-start(bf16[512,512]{1,0:T(8,128)(2,1)} %wm_ref.1) | copy-start | bytes 1572868
  4.5 2.1 %copy-start.2 = (bf16[512,512]{1,0:T(8,128)(2,1)S(1)}, bf16[512,512]{1,0:T(8,128)(2,1)}, u32[]{:S(2)}) copy-start(bf16[512,512]{1,0:T(8,128)(2,1)} %wu_ref.1) | copy-start | bytes 1572868
  4.5 2.1 %copy-start.3 = (bf16[256,512]{1,0:T(8,128)(2,1)S(1)}, bf16[256,512]{1,0:T(8,128)(2,1)}, u32[]{:S(2)}) copy-start(bf16[256,512]{1,0:T(8,128)(2,1)} %param.7) | copy-start | bytes 786436
  4.5 2.2 %copy-start.4 = (bf16[256,512]{1,0:T(8,128)(2,1)S(1)}, bf16[256,512]{1,0:T(8,128)(2,1)}, u32[]{:S(2)}) copy-start(bf16[256,512]{1,0:T(8,128)(2,1)} %cot_ref.1) | copy-start | bytes 786436
